TPU v7x, 32 devices: a whole 2x2x4 slice. The times are simulated.
32 devices in a mesh: teacher: 4 (over y, x), dp: 2 (over core), vocab: 4 (over z).
Axes of the slice: x: 2, y: 2, z: 4, core: 2. Of those that a mesh axis runs over, the one named last changes fastest.
Arguments:
- teacher_of_seq: int32 [16], replicated, may hold values from 0 to 3, as said below
- teacher_hidden: bfloat16 [4, 512, 4096], P('teacher', 'vocab', 'dp'), may hold values from -160 to 160, as said below
- teacher_weight: bfloat16 [4, 4096, 8192], P('teacher', 'dp', 'vocab'), may hold values from -0.09375 to 0.09375
- student_hidden: bfloat16 [1024, 3072], P(None, ('teacher', 'dp')), may hold values from -160 to 160
- student_weight: bfloat16 [3072, 8192], P(('teacher', 'dp'), 'vocab'), may hold values from -0.109375 to 0.109375
Outputs:
- kl_rows: float32 [1024], P(('teacher', 'dp'))
- grad_weight: bfloat16 [3072, 8192], P(('teacher', 'dp'), 'vocab')
- grad_hidden: bfloat16 [1024, 3072], P('vocab', ('teacher', 'dp'))
Inputs may be any that keep to these rules, and one draw needn't show every extreme that they name: `teacher_of_seq`: every teacher has at least one sequence and one teacher has exactly 8. `teacher_hidden`: slots from 64 times the teacher's number of sequences on are not read.
All inputs are finite; a program needn't handle non-finite values.
Results may differ from a plain program's by a relative error of at most 0.01225.
The roundings to bfloat16 on the way count: a program that leaves them out, or rounds other values in their place, can miss the bound.
Values may be sent and summed in bfloat16 or wider, within the bound.
A program may use at most 128 MiB of HBM per device.

v0:
```python
import jax
import jax.numpy as jnp
from jax import lax
from jax.sharding import PartitionSpec as P


def shards(teacher_of_seq, teacher_hidden, teacher_weight, student_hidden, student_weight):
    groups = lax.axis_size("teacher")
    dp_count = lax.axis_size("dp")
    owners = groups * dp_count
    team_index = lax.axis_index("teacher")
    dp_index = lax.axis_index("dp")
    vocab_cols = student_weight.shape[1]
    vocab_total = vocab_cols * lax.axis_size("vocab")
    row_count = student_hidden.shape[0]
    block_rows = row_count // owners
    seq_total = teacher_of_seq.shape[0]
    positions = row_count // seq_total
    slot_rows = teacher_hidden.shape[1] * lax.axis_size("vocab")
    half_slots = slot_rows // dp_count
    sequence_ids = jnp.arange(seq_total, dtype=jnp.int32)
    same_before = (teacher_of_seq[None, :] == teacher_of_seq[:, None]) & (
        sequence_ids[None, :] < sequence_ids[:, None]
    )
    earlier = jnp.sum(same_before.astype(jnp.int32), axis=1)
    all_rows = jnp.arange(row_count, dtype=jnp.int32)
    row_teacher_all = jnp.repeat(teacher_of_seq, positions)
    row_slot_all = jnp.repeat(earlier, positions) * positions + all_rows % positions
    gathered = lax.all_gather(teacher_hidden[0], "vocab", axis=0, tiled=True)
    weight_local = teacher_weight[0]
    slot_logits = lax.psum_scatter(
        jnp.dot(gathered, weight_local, preferred_element_type=jnp.float32),
        "dp",
        scatter_dimension=0,
        tiled=True,
    ).astype(jnp.bfloat16)
    local_slot = row_slot_all - dp_index * half_slots
    is_live = (row_teacher_all == team_index) & (local_slot >= 0) & (local_slot < half_slots)
    picked = jnp.take(slot_logits, jnp.clip(local_slot, 0, half_slots - 1), axis=0)
    buffer = jnp.where(is_live[:, None], picked, jnp.zeros_like(picked)).reshape(
        owners, block_rows, vocab_cols
    )
    received = lax.all_to_all(buffer, ("teacher", "dp"), split_axis=0, concat_axis=0, tiled=True)
    teacher_rows = jnp.sum(received.astype(jnp.float32), axis=0)
    student_logits = lax.psum_scatter(
        jnp.dot(student_hidden, student_weight, preferred_element_type=jnp.float32),
        ("teacher", "dp"),
        scatter_dimension=0,
        tiled=True,
    )
    teacher_top = lax.pmax(jnp.max(teacher_rows, axis=1), "vocab")
    teacher_total = lax.psum(jnp.sum(jnp.exp(teacher_rows - teacher_top[:, None]), axis=1), "vocab")
    teacher_lse = teacher_top + jnp.log(teacher_total)
    teacher_prob = jnp.exp(teacher_rows - teacher_lse[:, None])
    student_top = lax.pmax(jnp.max(student_logits, axis=1), "vocab")
    student_total, cross_term = lax.psum(
        (
            jnp.sum(jnp.exp(student_logits - student_top[:, None]), axis=1),
            jnp.sum(teacher_prob * (teacher_rows - student_logits), axis=1),
        ),
        "vocab",
    )
    student_lse = student_top + jnp.log(student_total)
    kl_rows = cross_term - teacher_lse + student_lse
    gradient = (
        vocab_total * (jnp.exp(student_logits - student_lse[:, None]) - teacher_prob)
    ).astype(jnp.bfloat16)
    everything = lax.all_gather(gradient, ("teacher", "dp"), axis=0, tiled=True)
    grad_weight = lax.dot_general(
        student_hidden, everything, (((0,), (0,)), ((), ())), preferred_element_type=jnp.float32
    ).astype(jnp.bfloat16)
    grad_hidden = lax.psum_scatter(
        lax.dot_general(
            everything, student_weight, (((1,), (1,)), ((), ())), preferred_element_type=jnp.float32
        ).astype(jnp.bfloat16),
        "vocab",
        scatter_dimension=0,
        tiled=True,
    )
    return (kl_rows, grad_weight, grad_hidden)


def solution(mesh):
    in_specs = (
        P(),
        P("teacher", "vocab", "dp"),
        P("teacher", "dp", "vocab"),
        P(None, ("teacher", "dp")),
        P(("teacher", "dp"), "vocab"),
    )
    out_specs = (P(("teacher", "dp")), P(("teacher", "dp"), "vocab"), P("vocab", ("teacher", "dp")))
    return jax.shard_map(shards, mesh=mesh, in_specs=in_specs, out_specs=out_specs, check_vma=False)
```

profile of v0, /device:TPU:7, one launch (start us, length us, event | category | flops | bytes accessed | tf_op | source)
XLA Modules:
  0.0 295.2 jit_solution(17625162220768336334)
XLA Ops:
  7.2 0.7 all-gather.6.cloned.1.call-update
  8.0 48.8 %all-gather.6.cloned.1.call-done = bf16[1,512,2048]{2,1,0:T(8,128)(2,1)} async-done(((bf16[1,128,2048]{2,1,0:T(8,128)(2,1)}), bf16[1,512,2048]{2,1,0:T(8,128)(2,1)}) %all-gather.6.cloned.1.call-update) | async-done | bytes 2097168 | tf_op jit(solution)/shard_map/all_gather | solution.py:29
  56.7 10.5 %fusion = f32[512,2048]{1,0:T(8,128)} fusion(bf16[1,2048,2048]{2,1,0:T(8,128)(2,1)} %param.7, bf16[1,512,2048]{2,1,0:T(8,128)(2,1)} %all-gather.6.cloned.1.call-done), kind=kOutput, calls=%fused_computation.1 | convolution fusion | flops 4294967296 | bytes 14680064 | tf_op jit(solution)/shard_map/dot_general | solution.py:32
  67.3 1.0 copy-done.1
  68.3 5.9 %fusion.11 = f32[1024,2048]{1,0:T(8,128)} fusion(bf16[1024,384]{1,0:T(8,128)(2,1)S(1)} %copy-done.1, bf16[384,2048]{1,0:T(8,128)(2,1)S(1)} %copy-done), kind=kOutput, calls=%fused_computation.36 | convolution fusion | flops 1610612736 | bytes 10747904 | tf_op jit(solution)/shard_map/dot_general | solution.py:46
  74.2 0.6 copy-done.2
  75.8 3.2 %reduce-scatter.4.cloned.1.call-done = f32[256,2048]{1,0:T(8,128)} async-done(((f32[512,2048]{1,0:T(8,128)}), f32[256,2048]{1,0:T(8,128)}) %reduce-scatter.4.cloned.1.call-update) | async-done | bytes 2097168 | tf_op jit(solution)/shard_map/reduce_scatter | solution.py:31
  78.9 1.7 convert_element_type.22
  80.7 6.0 %gather_fusion = bf16[1024,2048]{1,0:T(8,128)(2,1)} fusion(bf16[256,2048]{1,0:T(8,128)(2,1)S(1)} %convert_element_type.22, s32[1024]{0:T(1024)S(1)} %broadcast_clamp_fusion), kind=kCustom, calls=%fused_computation | custom fusion | bytes 8392704 | tf_op jit(solution)/shard_map/jit(_take)/gather | solution.py:39
  86.7 3.9 %select_select_fusion = bf16[8,128,2048]{2,1,0:T(8,128)(2,1)} fusion(bf16[8,128,2048]{2,1,0:T(8,128)(2,1)} %bitcast.16, pred[8,128]{1,0:T(8,128)(4,1)S(1)} %get-tuple-element.21, pred[8,128]{1,0:T(8,128)(4,1)S(1)} %get-tuple-element.20), kind=kLoop, calls=%fused_computation.4 | loop fusion | flops 4194304 | bytes 8390656 | tf_op jit(solution)/shard_map/jit(_where)/select_n | solution.py:40
  90.6 4.7 %all-to-all-start = ((bf16[8,128,2048]{2,1,0:T(8,128)(2,1)}), bf16[8,128,2048]{2,1,0:T(8,128)(2,1)}, u32[]{:S(2)}, u32[]{:S(2)}) async-start(bf16[8,128,2048]{2,1,0:T(8,128)(2,1)} %select_select_fusion), calls=%async_computation.1 | async-start | bytes 8388608 | tf_op jit(solution)/shard_map/all_to_all | solution.py:43
  95.4 90.8 %reduce-scatter.6.cloned.1.call-done = f32[128,2048]{1,0:T(8,128)} async-done(((f32[1024,2048]{1,0:T(8,128)}), f32[128,2048]{1,0:T(8,128)}) %reduce-scatter.6.cloned.1.call-update) | async-done | bytes 1048592 | tf_op jit(solution)/shard_map/reduce_scatter | solution.py:45
  186.1 1.4 reduce_max.19
  187.5 3.0 %convert_reduce_fusion = f32[128,2048]{1,0:T(8,128)S(1)} fusion(bf16[8,128,2048]{2,1,0:T(8,128)(2,1)} %all-to-all-done), kind=kLoop, calls=%fused_computation.3 | loop fusion | flops 3932160 | bytes 5242880 | tf_op jit(solution)/shard_map/reduce_sum | solution.py:44
  190.7 9.6 %all-reduce.1 = (f32[128]{0:T(128)S(1)}, f32[128]{0:T(128)S(1)}) all-reduce(f32[128]{0:T(128)S(1)} %reduce_max.19, f32[128]{0:T(128)S(1)} %reduce_max.18), channel_id=1, replica_groups=mesh['teacher'=4,'dp'=2,'vocab'=4] {'vocab'}, use_global_device_ids=true, to_apply=%region_11.12 | all-reduce | flops 256 | bytes 2048 | tf_op jit(solution)/shard_map/pmax | solution.py:55
  200.6 6.6 %psum.21 = f32[128]{0:T(128)S(1)} all-reduce(f32[128]{0:T(128)S(1)} %exponential_reduce_fusion.1), channel_id=1, replica_groups=mesh['teacher'=4,'dp'=2,'vocab'=4] {'vocab'}, use_global_device_ids=true, to_apply=%region_6.7 | all-reduce | flops 128 | bytes 1024 | tf_op jit(solution)/shard_map/psum | solution.py:52
  207.2 1.7 multiply_reduce_fusion
  208.9 8.4 %all-reduce = (f32[128]{0:T(128)S(1)}, f32[128]{0:T(128)S(1)}) all-reduce(f32[128]{0:T(128)S(1)} %get-tuple-element.13, f32[128]{0:T(128)S(1)} %get-tuple-element.12), channel_id=1, replica_groups=mesh['teacher'=4,'dp'=2,'vocab'=4] {'vocab'}, use_global_device_ids=true, to_apply=%region_13.14 | all-reduce | flops 256 | bytes 2048 | tf_op jit(solution)/shard_map/psum | solution.py:56
  217.8 2.4 multiply_convert_fusion
  220.5 40.1 %all-gather.4.cloned.1.call-done = bf16[1024,2048]{1,0:T(8,128)(2,1)} async-done(((bf16[128,2048]{1,0:T(8,128)(2,1)}), bf16[1024,2048]{1,0:T(8,128)(2,1)}) %all-gather.4.cloned.1.call-update) | async-done | bytes 4194320 | tf_op jit(solution)/shard_map/all_gather | solution.py:68
  260.5 5.4 %convolution_convert_fusion.1 = bf16[1024,384]{1,0:T(8,128)(2,1)} fusion(bf16[1024,2048]{1,0:T(8,128)(2,1)} %all-gather.4.cloned.1.call-done, bf16[384,2048]{1,0:T(8,128)(2,1)S(1)} %copy-done), kind=kOutput, calls=%fused_computation.8 | convolution fusion | flops 1611005952 | bytes 6553600 | tf_op jit(solution)/shard_map/dot_general | solution.py:73
  266.0 4.8 %fusion.2 = bf16[384,2048]{0,1:T(8,128)(2,1)S(1)} fusion(bf16[1024,2048]{1,0:T(8,128)(2,1)} %all-gather.4.cloned.1.call-done, bf16[1024,384]{1,0:T(8,128)(2,1)} %param.8), kind=kOutput, calls=%fused_computation.6 | convolution fusion | flops 1611399168 | bytes 6553600 | tf_op jit(solution)/shard_map/dot_general | solution.py:69
  270.8 1.6 copy.10
  272.4 16.3 %reduce-scatter.8.cloned.1.call-done = bf16[256,384]{1,0:T(8,128)(2,1)} async-done(((bf16[1024,384]{1,0:T(8,128)(2,1)}), bf16[256,384]{1,0:T(8,128)(2,1)}) %reduce-scatter.8.cloned.1.call-update) | async-done | bytes 196624 | tf_op jit(solution)/shard_map/reduce_scatter | solution.py:72
  (32 shorter events, 2.3 us)
Async XLA Ops:
  7.2 60.1 %copy-start = (bf16[384,2048]{1,0:T(8,128)(2,1)S(1)}, bf16[384,2048]{1,0:T(8,128)(2,1)}, u32[]{:S(2)}) copy-start(bf16[384,2048]{1,0:T(8,128)(2,1)} %param.9) | copy-start | bytes 4718596
  7.2 49.5 %all-gather.6.cloned.1.call-start = ((), (), s32[]{:S(2)}) async-start(), calls=%async_computation.8 | async-start | bytes 2621440 | tf_op jit(solution)/shard_map/all_gather | solution.py:29
  7.9 71.0 %reduce-scatter.4.cloned.1.call-start = ((), (), s32[]{:S(2)}) async-start(), calls=%async_computation.4 | async-start | bytes 6291456 | tf_op jit(solution)/shard_map/reduce_scatter | solution.py:31
  67.2 1.1 copy-start.1
  67.2 118.9 %reduce-scatter.6.cloned.1.call-start = ((), (), s32[]{:S(2)}) async-start(), calls=%async_computation.5 | async-start | bytes 9437184 | tf_op jit(solution)/shard_map/reduce_scatter | solution.py:45
  74.2 0.7 copy-start.2
  90.6 96.9 %all-to-all-start = ((bf16[8,128,2048]{2,1,0:T(8,128)(2,1)}), bf16[8,128,2048]{2,1,0:T(8,128)(2,1)}, u32[]{:S(2)}, u32[]{:S(2)}) async-start(bf16[8,128,2048]{2,1,0:T(8,128)(2,1)} %select_select_fusion), calls=%async_computation.1 | async-start | bytes 8388608 | tf_op jit(solution)/shard_map/all_to_all | solution.py:43
  95.3 165.2 %all-gather.4.cloned.1.call-start = ((), (), s32[]{:S(2)}) async-start(), calls=%async_computation.6 | async-start | bytes 4718592 | tf_op jit(solution)/shard_map/all_gather | solution.py:68
  220.3 68.4 %reduce-scatter.8.cloned.1.call-start = ((), (), s32[]{:S(2)}) async-start(), calls=%async_computation.7 | async-start | bytes 983040 | tf_op jit(solution)/shard_map/reduce_scatter | solution.py:72
Sparse Core Ops, SparseCore 0:
  9.6 47.0 all-gather.5
  67.4 11.5 reduce-scatter.3
  82.8 103.3 reduce-scatter.5
  220.4 40.1 all-gather.3
  266.1 22.4 reduce-scatter.7
where the time goes:
time: 299 us; the launch traced here: 295 us
  waiting for transfers between devices  200 us (67%)
  matrix products  26.5 us (9%)
  blocking collectives  24.7 us (8%)
  other arithmetic  15.3 us (5%)
  between operations  13.8 us (5%)
  local copies, waits for them, and re-layouts  9.98 us (3%)
  starting transfers between devices  5.07 us (2%)
    reduce_scatter x1, waiting for transfers between devices, shards(): lax.psum_scatter(jnp.dot(student_hidden, student_weight, preferred_elemen...  90.8 us
    all_gather x1, waiting for transfers between devices, shards(): gathered = lax.all_gather(teacher_hidden[0], 'vocab', axis=0, tiled=True)  48.8 us
    all_gather x1, waiting for transfers between devices, shards(): everything = lax.all_gather(gradient, ('teacher', 'dp'), axis=0, tiled=True)  40.1 us
    reduce_scatter x1, waiting for transfers between devices, shards(): lax.psum_scatter(lax.dot_general(everything, student_weight, (((1,), (1,)...  16.3 us
    dot_general x1, matrix products, shards(): jnp.dot(gathered, weight_local, preferred_element_type=jnp.float32)  10.5 us
    pmax x1, blocking collectives, shards(): student_top = lax.pmax(jnp.max(student_logits, axis=1), 'vocab')  9.64 us
    psum x1, blocking collectives, shards(): lax.psum((jnp.sum(jnp.exp(student_logits - student_top[:, None]), axis=1)...  8.38 us
    psum x1, blocking collectives, shards(): lax.psum(jnp.sum(jnp.exp(teacher_rows - teacher_top[:, None]), axis=1), '...  6.63 us
  transfers between devices with their start and end apart: 6, of which 5 were waited for; matrix products, arithmetic and copies ran while one was open for 9% of the time, Pallas kernels for 0%

commit v1 on v0

v1 whole, which is shorter than its diff:
```python
import functools

import jax
import jax.numpy as jnp
from jax import lax
from jax.experimental import pallas as pl
from jax.experimental.pallas import tpu as pltpu
from jax.sharding import PartitionSpec as P

MESH = pl.DeviceIdType.MESH
F32 = jnp.float32
BF16 = jnp.bfloat16


def kernel(
    Z, vocab_total,
    pick_ref, hidden_ref, head_ref, x_ref, w_ref,
    kl_ref, gw_ref, gh_ref,
    head, th, ph, work, s_rx, s_r1, s_r2, t_rx, t_sum, t_r1, t_r2, xt, st, tile, g_all, ghp, gh_rx,
    head_sem, z_send, z_recv,
    sc_send, sc_recv, s1_send, s1_recv, s2_send, s2_recv,
    tc_send, tc_recv, t1_send, t1_recv, t2_send, t2_recv,
    st_send, st_recv, g_send, g_recv, gc_send, gc_recv, gh_send, gh_recv,
):
    t = lax.axis_index("teacher")
    c = lax.axis_index("dp")
    z = lax.axis_index("vocab")
    low = lax.rem(t, 2)
    high = lax.div(t, 2)
    mates = (t, t + 1 - 2 * low, t + 2 - 4 * high, 3 - t)
    other = 1 - c
    devs = tuple((m, c, z) for m in mates)
    core = (t, other, z)
    rows, cols = s_r2.shape
    half = cols // 2
    cut = (pl.ds(0, half), pl.ds(half, half))
    zrows = hidden_ref.shape[0]
    hrows = gh_ref.shape[0]

    def at(block, count):
        return pl.ds(pl.multiple_of(block * count, count), count)

    def remote(src, dst, send, recv, dev):
        return pltpu.make_async_remote_copy(
            src_ref=src, dst_ref=dst, send_sem=send, recv_sem=recv, device_id=dev, device_id_type=MESH
        )

    barrier = pltpu.get_barrier_semaphore()
    for dev in (core, devs[1], devs[2]):
        pl.semaphore_signal(barrier, inc=1, device_id=dev, device_id_type=MESH)
    for dz in range(1, Z):
        pl.semaphore_signal(barrier, inc=1, device_id=(t, c, lax.rem(z + dz, Z)), device_id_type=MESH)
    head_copy = pltpu.make_async_copy(head_ref, head, head_sem)
    head_copy.start()
    th[at(z, zrows), :] = hidden_ref[...]
    pl.semaphore_wait(barrier, 2 + Z)

    def z_copy(block, way, step, target):
        return remote(
            th.at[at(block, zrows)], th.at[at(block, zrows)], z_send.at[way, step], z_recv.at[block], (t, c, target)
        )

    def z_start(step):
        @pl.when((z - step >= 0) & (z + 1 < Z))
        def _():
            z_copy(z - step, 0, step, z + 1).start()

        @pl.when((z + step < Z) & (z >= 1))
        def _():
            z_copy(z + step, 1, step, z - 1).start()

    def z_wait(step):
        @pl.when(z - 1 - step >= 0)
        def _():
            z_copy(z - 1 - step, 0, step, z - 1).wait_recv()

        @pl.when(z + 1 + step < Z)
        def _():
            z_copy(z + 1 + step, 1, step, z + 1).wait_recv()

    def z_end(step):
        @pl.when((z - step >= 0) & (z + 1 < Z))
        def _():
            z_copy(z - step, 0, step, z + 1).wait_send()

        @pl.when((z + step < Z) & (z >= 1))
        def _():
            z_copy(z + step, 1, step, z - 1).wait_send()

    def owner(j, which):
        return 2 * mates[j] + which

    def first_hop(j, summed, r1, sems):
        send, recv = sems
        copies = []
        if j == 3:
            for h in (0, 1):
                copies.append(
                    remote(summed.at[3, :, cut[h]], r1.at[0, :, cut[h]], send.at[0, h], recv.at[0, h], devs[1 + h])
                )
        elif j in (1, 2):
            h = j - 1
            copies.append(
                remote(summed.at[j, :, cut[h]], r1.at[1, :, cut[h]], send.at[1, h], recv.at[1, h], devs[j])
            )
        for copy in copies:
            copy.start()
        return copies

    def second_hop(h, first, summed, r1, r2, sems):
        send, recv = sems
        j = 2 - h
        first[h].wait_recv()
        summed[j, :, cut[h]] = (
            summed[j, :, cut[h]].astype(F32) + r1[0, :, cut[h]].astype(F32)
        ).astype(summed.dtype)
        copy = remote(summed.at[j, :, cut[h]], r2.at[:, cut[h]], send.at[h], recv.at[h], devs[j])
        copy.start()
        return copy

    ORDER = (3, 1, 2, 0)
    z_start(0)
    pair = {}
    for j in ORDER:
        work[j, other] = jnp.dot(x_ref[at(owner(j, other), rows), :], w_ref[...], preferred_element_type=F32)
        pair[j] = remote(work.at[j, other], s_rx.at[j], sc_send.at[j], sc_recv.at[j], core)
        pair[j].start()
    s_first = []
    for j in ORDER:
        mine = jnp.dot(x_ref[at(owner(j, c), rows), :], w_ref[...], preferred_element_type=F32)
        pair[j].wait_recv()
        s_rx[j] = s_rx[j] + mine
        s_first += first_hop(j, s_rx, s_r1, (s1_send, s1_recv))
    xt[...] = x_ref[...].T
    for step in range(Z - 1):
        z_wait(step)
        if step + 1 < Z - 1:
            z_start(step + 1)
        if step == 0:
            s_second = [second_hop(h, s_first, s_rx, s_r1, s_r2, (s2_send, s2_recv)) for h in (0, 1)]
    head_copy.wait()

    for j in ORDER:
        pair[j].wait_send()
    chunk = cols // 8
    tpair = {}
    for j in ORDER:
        ph[...] = jnp.dot(
            pick_ref[at(mates[j], 2 * rows), :], th[...], preferred_element_type=F32
        ).astype(BF16)

        @pl.loop(0, 8)
        def _(i, j=j):
            where = at(i, chunk)
            part = jnp.dot(ph[...], head[:, where], preferred_element_type=F32)
            work[j, 0, :, where] = part[:rows]
            work[j, 1, :, where] = part[rows:]

        tpair[j] = remote(work.at[j, other], t_rx.at[j], tc_send.at[j], tc_recv.at[j], core)
        tpair[j].start()
    t_first = []
    for j in ORDER:
        tpair[j].wait_recv()
        t_sum[j] = (t_rx[j] + work[j, c]).astype(BF16)
        t_first += first_hop(j, t_sum, t_r1, (t1_send, t1_recv))
    t_second = [second_hop(h, t_first, t_sum, t_r1, t_r2, (t2_send, t2_recv)) for h in (0, 1)]

    s_first[2].wait_recv()
    s_first[3].wait_recv()
    for h in (0, 1):
        s_second[h].wait_recv()
    s_rx[0] = s_rx[0] + s_r1[1] + s_r2[...]
    student = s_rx[0]
    s_top = jnp.max(student, axis=1, keepdims=True)
    s_total = jnp.sum(jnp.exp(student - s_top), axis=1, keepdims=True)
    t_first[2].wait_recv()
    t_first[3].wait_recv()
    for h in (0, 1):
        t_second[h].wait_recv()
    t_sum[0] = (t_sum[0].astype(F32) + t_r1[1].astype(F32) + t_r2[...].astype(F32)).astype(BF16)
    teacher = t_sum[0].astype(F32)
    t_top = jnp.max(teacher, axis=1, keepdims=True)
    t_exp = jnp.exp(teacher - t_top)
    t_total = jnp.sum(t_exp, axis=1, keepdims=True)
    cross = jnp.sum(t_exp * (teacher - s_rx[0]), axis=1, keepdims=True)
    lane = lax.broadcasted_iota(jnp.int32, tile.shape, 1)
    packed = jnp.zeros(tile.shape, F32)
    for k, column in enumerate((t_top, t_total, s_top, s_total, cross)):
        packed = jnp.where(lane == k, column, packed)
    st[z] = packed.T[:8, :]
    st_out = []
    for dz in range(1, Z):
        copy = remote(st.at[z], st.at[z], st_send.at[dz], st_recv.at[z], (t, c, lax.rem(z + dz, Z)))
        copy.start()
        st_out.append(copy)
    for dz in range(1, Z):
        source = lax.rem(z + dz, Z)
        remote(st.at[source], st.at[source], st_send.at[dz], st_recv.at[source], (t, c, source)).wait_recv()
    every = [st[k] for k in range(Z)]
    t_top = functools.reduce(jnp.maximum, [e[0:1] for e in every])
    s_top = functools.reduce(jnp.maximum, [e[2:3] for e in every])
    t_total = sum(e[1:2] * jnp.exp(e[0:1] - t_top) for e in every)
    s_total = sum(e[3:4] * jnp.exp(e[2:3] - s_top) for e in every)
    t_lse = t_top + jnp.log(t_total)
    s_lse = s_top + jnp.log(s_total)
    cross = sum(e[4:5] * jnp.exp(e[0:1] - t_lse) for e in every)
    kl = cross - t_lse + s_lse
    kl_ref[...] = jnp.broadcast_to(kl, kl_ref.shape)
    line = lax.broadcasted_iota(jnp.int32, tile.shape, 0)
    tile[...] = jnp.where(line == 0, t_lse, jnp.where(line == 1, s_lse, 0.0)).T
    t_lse = tile[:, 0:1]
    s_lse = tile[:, 1:2]
    me = owner(0, c)
    g_all[at(me, rows), :] = (
        vocab_total * (jnp.exp(s_rx[0] - s_lse) - jnp.exp(t_sum[0].astype(F32) - t_lse))
    ).astype(BF16)

    def g_copy(j, which, sems, k, dev, columns=pl.ds(0, cols)):
        ref = g_all.at[at(owner(j, which), rows), columns]
        return remote(ref, ref, sems[0].at[k], sems[1].at[k], dev)

    chips, cores = (g_send, g_recv), (gc_send, gc_recv)
    sent = [g_copy(0, c, chips, 0, devs[1]), g_copy(0, c, chips, 1, devs[2]), g_copy(0, c, cores, 0, core)]
    for copy in sent:
        copy.start()

    def arrived(j, k, columns=pl.ds(0, cols)):
        g_copy(j, c, chips, k, devs[1], columns).wait_recv()

    def forward(j, sems, k, dev, columns=pl.ds(0, cols)):
        copy = g_copy(j, c, sems, k, dev, columns)
        copy.start()
        sent.append(copy)

    gh_out = []

    def hidden_rows(j):
        g_copy(j, other, cores, j, core).wait_recv()
        where = at(mates[j], 2 * rows)
        ghp[where, :] = lax.dot_general(
            g_all[where, :], w_ref[...], (((1,), (1,)), ((), ())), preferred_element_type=F32
        ).astype(BF16)
        for q in range(Z // 4):
            target = mates[j] * (Z // 4) + q
            copy = remote(
                ghp.at[at(target, hrows)], gh_rx.at[z], gh_send.at[j * (Z // 4) + q], gh_recv.at[z], (t, c, target)
            )
            gh_out.append((target, copy))

            @pl.when(target != z)
            def _(copy=copy):
                copy.start()

    arrived(1, 0)
    forward(1, chips, 2, devs[2], cut[0])
    forward(1, cores, 1, core)
    arrived(2, 1)
    forward(2, chips, 3, devs[1], cut[1])
    forward(2, cores, 2, core)
    hidden_rows(0)
    hidden_rows(1)
    hidden_rows(2)
    arrived(3, 2, cut[0])
    arrived(3, 3, cut[1])
    forward(3, cores, 3, core)
    hidden_rows(3)

    wide = cols // 4
    @pl.loop(0, 4)
    def _(i):
        where = at(i, wide)
        gw_ref[:, where] = jnp.dot(xt[...], g_all[:, where], preferred_element_type=F32).astype(BF16)

    total = ghp[at(z, hrows), :].astype(F32)
    for dz in range(1, Z):
        source = lax.rem(z + dz, Z)
        remote(
            ghp.at[at(source, hrows)], gh_rx.at[source], gh_send.at[0], gh_recv.at[source], (t, c, source)
        ).wait_recv()
        total = total + gh_rx[source].astype(F32)
    gh_ref[...] = total.astype(BF16)

    for target, copy in gh_out:
        @pl.when(target != z)
        def _(copy=copy):
            copy.wait_send()
    for copy in sent + st_out + s_first + s_second + t_first + t_second:
        copy.wait_send()
    for j in ORDER:
        tpair[j].wait_send()
    for step in range(Z - 1):
        z_end(step)


def shards(teacher_of_seq, teacher_hidden, teacher_weight, student_hidden, student_weight):
    Z = lax.axis_size("vocab")
    owners = lax.axis_size("teacher") * lax.axis_size("dp")
    cols = student_weight.shape[1]
    row_count, features = student_hidden.shape
    rows = row_count // owners
    seqs = teacher_of_seq.shape[0]
    positions = row_count // seqs
    ids = jnp.arange(seqs, dtype=jnp.int32)
    same = (teacher_of_seq[None, :] == teacher_of_seq[:, None]) & (ids[None, :] < ids[:, None])
    zrows, width = teacher_hidden.shape[1:]
    all_rows = jnp.arange(row_count, dtype=jnp.int32)
    slot = jnp.repeat(jnp.sum(same.astype(jnp.int32), axis=1), positions) * positions + all_rows % positions
    live = jnp.repeat(teacher_of_seq == lax.axis_index("teacher"), positions)
    slot_ids = jnp.arange(zrows * Z, dtype=jnp.int32)
    pick = ((slot[:, None] == slot_ids[None, :]) & live[:, None]).astype(BF16)
    hrows = row_count // Z
    dma = pltpu.SemaphoreType.DMA
    vmem = pl.BlockSpec(memory_space=pltpu.VMEM)
    hop_sems = [dma((4,)), dma((4,)), dma((2, 2)), dma((2, 2)), dma((2,)), dma((2,))]
    kl, grad_weight, grad_hidden = pl.pallas_call(
        functools.partial(kernel, Z, float(cols * Z)),
        out_shape=(
            jax.ShapeDtypeStruct((8, rows), F32),
            jax.ShapeDtypeStruct((features, cols), BF16),
            jax.ShapeDtypeStruct((hrows, features), BF16),
        ),
        in_specs=[vmem, vmem, pl.BlockSpec(memory_space=pl.ANY), vmem, vmem],
        out_specs=(vmem, vmem, vmem),
        scratch_shapes=[
            pltpu.VMEM((width, cols), BF16),
            pltpu.VMEM((zrows * Z, width), BF16),
            pltpu.VMEM((2 * rows, width), BF16),
            pltpu.VMEM((4, 2, rows, cols), F32),
            pltpu.VMEM((4, rows, cols), F32),
            pltpu.VMEM((2, rows, cols), F32),
            pltpu.VMEM((rows, cols), F32),
            pltpu.VMEM((4, rows, cols), F32),
            pltpu.VMEM((4, rows, cols), BF16),
            pltpu.VMEM((2, rows, cols), BF16),
            pltpu.VMEM((rows, cols), BF16),
            pltpu.VMEM((features, row_count), BF16),
            pltpu.VMEM((Z, 8, rows), F32),
            pltpu.VMEM((rows, rows), F32),
            pltpu.VMEM((row_count, cols), BF16),
            pltpu.VMEM((row_count, features), BF16),
            pltpu.VMEM((Z, hrows, features), BF16),
            dma(()), dma((2, Z)), dma((Z,)),
            *hop_sems, *hop_sems,
            dma((Z,)), dma((Z,)), dma((4,)), dma((4,)), dma((4,)), dma((4,)), dma((Z,)), dma((Z,)),
        ],
        compiler_params=pltpu.CompilerParams(
            collective_id=0, has_side_effects=True, vmem_limit_bytes=60 * 1024 * 1024
        ),
    )(pick, teacher_hidden[0], teacher_weight[0], student_hidden, student_weight)
    return (kl[0], grad_weight, grad_hidden)


def solution(mesh):
    in_specs = (
        P(),
        P("teacher", "vocab", "dp"),
        P("teacher", "dp", "vocab"),
        P(None, ("teacher", "dp")),
        P(("teacher", "dp"), "vocab"),
    )
    out_specs = (P(("teacher", "dp")), P(("teacher", "dp"), "vocab"), P("vocab", ("teacher", "dp")))
    return jax.shard_map(shards, mesh=mesh, in_specs=in_specs, out_specs=out_specs, check_vma=False)
```

time: 299 us -> 126 us (0.42); the launches traced: 295 us -> 126 us
  waiting for transfers between devices: 200 us -> 0 us
  Pallas kernels: 0 us -> 117 us
  matrix products: 26.5 us -> 0 us
  blocking collectives: 24.7 us -> 0 us
  between operations: 13.8 us -> 0.66 us
  other arithmetic: 15.3 us -> 3.16 us
  starting transfers between devices: 5.07 us -> 0 us
  local copies, waits for them, and re-layouts: 9.98 us -> 4.94 us
    pallas_call x0 -> x1, Pallas kernels: none -> 117 us  [shards(): pl.pallas_call(functools.partial(kernel, Z, float(cols * Z)), out_shape=(...]
    reduce_scatter x3 -> x0, waiting for transfers between devices: 110 us -> none  [the longest x1 90.8 us: shards(): lax.psum_scatter(jnp.dot(student_hidden, student_weight, preferred_elemen...]
    all_gather x2 -> x0, waiting for transfers between devices: 88.8 us -> none  [the longest x1 48.8 us: shards(): gathered = lax.all_gather(teacher_hidden[0], 'vocab', axis=0, tiled=True)]
    dot_general x4 -> x0, matrix products: 26.5 us -> none  [the longest x1 10.5 us: shards(): jnp.dot(gathered, weight_local, preferred_element_type=jnp.float32)]
    psum x2 -> x0, blocking collectives: 15 us -> none  [the longest x1 8.38 us: shards(): lax.psum((jnp.sum(jnp.exp(student_logits - student_top[:, None]), axis=1)...]
    pmax x1 -> x0, blocking collectives: 9.64 us -> none  [shards(): student_top = lax.pmax(jnp.max(student_logits, axis=1), 'vocab')]
    gather x1 -> x0, local copies, waits for them, and re-layouts: 6.02 us -> none  [shards(): jnp.take(slot_logits, jnp.clip(local_slot, 0, half_slots - 1), axis=0)]
    all_to_all x1 -> x0, starting transfers between devices: 4.72 us -> none  [shards(): lax.all_to_all(buffer, ('teacher', 'dp'), split_axis=0, concat_axis=0, ti...]
  transfers between devices with their start and end apart: 6 -> 0, of which waited for: 5 -> 0; matrix products, arithmetic and copies ran while one was open for 9% -> 0% of each run, Pallas kernels for 0% -> 0%
where the time goes in v1:
time: 126 us
  Pallas kernels  117 us (93%)
  local copies, waits for them, and re-layouts  4.94 us (4%)
  other arithmetic  3.16 us (3%)
    pallas_call x1, Pallas kernels, shards(): pl.pallas_call(functools.partial(kernel, Z, float(cols * Z)), out_shape=(...  117 us
    unnamed x4, local copies, waits for them, and re-layouts  3.41 us

profile of v1, /device:TPU:7, one launch (start us, length us, event | category | flops | bytes accessed | tf_op | source)
XLA Modules:
  0.0 125.7 jit_solution(2264016377961327799)
XLA Ops:
  0.6 0.7 broadcast_compare_fusion
  1.3 0.9 convert_reduce_fusion
  2.2 0.1 broadcast_in_dim.5
  2.3 0.1 and.28
  2.4 0.1 broadcast_in_dim.4
  2.4 0.1 mul.18
  2.5 1.6 %fusion.1.pick_ref = bf16[1024,512]{1,0:T(8,128)(2,1)} fusion(s32[1024]{0:T(1024)S(1)} %fusion.3, pred[1024]{0:T(1024)(128)(4,1)S(1)} %and.28), kind=kLoop, calls=%fused_computation.2 | loop fusion | flops 1572864 | bytes 1053696 | tf_op jit(solution)/shard_map/convert_element_type | solution.py:310
  4.1 116.9 %shard_map.76 = (f32[8,128]{1,0:T(8,128)}, bf16[384,2048]{1,0:T(8,128)(2,1)}, bf16[256,384]{1,0:T(8,128)(2,1)}) custom-call(bf16[1024,512]{1,0:T(8,128)(2,1)} %fusion.1.pick_ref, bf16[128,2048]{1,0:T(8,128)(2,1)} %bitcast.5, bf16[2048,2048]{1,0:T(8,128)(2,1)} %bitcast.4, bf16[1024,384]{1,0:T(8,128)(2,1)} %x_ref.1, bf16[384,2048]{1,0:T(8,128)(2,1)} %w_ref.1), custom_call_target="tpu_custom_call" | custom-call | tf_op jit(solution)/shard_map/pallas_call | solution.py:315
  121.0 0.0 copy-start
  121.0 1.2 slice_bitcast_fusion
  122.3 2.7 %copy.10 = bf16[384,2048]{1,0:T(8,128)(2,1)} copy(bf16[384,2048]{1,0:T(8,128)(2,1)} %get-tuple-element.13) | data formatting | bytes 3145728
  125.0 0.0 copy-done
  125.0 0.7 copy.11
  (2 shorter events, 0.0 us)
Async XLA Ops:
  121.0 4.0 %copy-start = (bf16[256,384]{1,0:T(8,128)(2,1)S(1)}, bf16[256,384]{1,0:T(8,128)(2,1)}, u32[]{:S(2)}) copy-start(bf16[256,384]{1,0:T(8,128)(2,1)} %get-tuple-element.14) | copy-start | bytes 589828

commit v2 on v1

--- a/solution.py
+++ b/solution.py
@@ -16,11 +16,11 @@
     Z, vocab_total,
     pick_ref, hidden_ref, head_ref, x_ref, w_ref,
     kl_ref, gw_ref, gh_ref,
-    head, th, ph, work, s_rx, s_r1, s_r2, t_rx, t_sum, t_r1, t_r2, xt, st, tile, g_all, ghp, gh_rx,
+    head, th, ph, work, s_rx, s_r1, s_r2, t_rx, t_sum, t_r1, t_r2, xp, xt, kl_mine, kl_all, st, tile, g_all, ghp, gh_rx,
     head_sem, z_send, z_recv,
     sc_send, sc_recv, s1_send, s1_recv, s2_send, s2_recv,
     tc_send, tc_recv, t1_send, t1_recv, t2_send, t2_recv,
-    st_send, st_recv, g_send, g_recv, gc_send, gc_recv, gh_send, gh_recv,
+    st_send, st_recv, g_send, g_recv, gc_send, gc_recv, gh_send, gh_recv, kl_send, kl_recv,
 ):
     t = lax.axis_index("teacher")
     c = lax.axis_index("dp")
@@ -36,6 +36,9 @@
     cut = (pl.ds(0, half), pl.ds(half, half))
     zrows = hidden_ref.shape[0]
     hrows = gh_ref.shape[0]
+    unit = rows // 4
+    piece = min(2 * unit, hrows)
+    mine_at = 2 * low + c
 
     def at(block, count):
         return pl.ds(pl.multiple_of(block * count, count), count)
@@ -46,14 +49,14 @@
         )
 
     barrier = pltpu.get_barrier_semaphore()
-    for dev in (core, devs[1], devs[2]):
+    for dev in (core, *devs[1:], *((m, other, z) for m in mates[1:])):
         pl.semaphore_signal(barrier, inc=1, device_id=dev, device_id_type=MESH)
     for dz in range(1, Z):
         pl.semaphore_signal(barrier, inc=1, device_id=(t, c, lax.rem(z + dz, Z)), device_id_type=MESH)
     head_copy = pltpu.make_async_copy(head_ref, head, head_sem)
     head_copy.start()
     th[at(z, zrows), :] = hidden_ref[...]
-    pl.semaphore_wait(barrier, 2 + Z)
+    pl.semaphore_wait(barrier, 6 + Z)
 
     def z_copy(block, way, step, target):
         return remote(
@@ -120,18 +123,23 @@
 
     ORDER = (3, 1, 2, 0)
     z_start(0)
+    for o in range(8):
+        for q in range(4):
+            xp[o * rows + q * unit:o * rows + (q + 1) * unit, :] = x_ref[
+                (q * 8 + o) * unit:(q * 8 + o + 1) * unit, :
+            ]
     pair = {}
     for j in ORDER:
-        work[j, other] = jnp.dot(x_ref[at(owner(j, other), rows), :], w_ref[...], preferred_element_type=F32)
+        work[j, other] = jnp.dot(xp[at(owner(j, other), rows), :], w_ref[...], preferred_element_type=F32)
         pair[j] = remote(work.at[j, other], s_rx.at[j], sc_send.at[j], sc_recv.at[j], core)
         pair[j].start()
     s_first = []
     for j in ORDER:
-        mine = jnp.dot(x_ref[at(owner(j, c), rows), :], w_ref[...], preferred_element_type=F32)
+        mine = jnp.dot(xp[at(owner(j, c), rows), :], w_ref[...], preferred_element_type=F32)
         pair[j].wait_recv()
         s_rx[j] = s_rx[j] + mine
         s_first += first_hop(j, s_rx, s_r1, (s1_send, s1_recv))
-    xt[...] = x_ref[...].T
+    xt[...] = xp[...].T
     for step in range(Z - 1):
         z_wait(step)
         if step + 1 < Z - 1:
@@ -144,7 +152,14 @@
         pair[j].wait_send()
     chunk = cols // 8
     tpair = {}
-    for j in ORDER:
+    t_first = []
+
+    def teacher_rows(j):
+        tpair[j].wait_recv()
+        t_sum[j] = (t_rx[j] + work[j, c]).astype(BF16)
+        return first_hop(j, t_sum, t_r1, (t1_send, t1_recv))
+
+    for n, j in enumerate(ORDER):
         ph[...] = jnp.dot(
             pick_ref[at(mates[j], 2 * rows), :], th[...], preferred_element_type=F32
         ).astype(BF16)
@@ -158,11 +173,9 @@
 
         tpair[j] = remote(work.at[j, other], t_rx.at[j], tc_send.at[j], tc_recv.at[j], core)
         tpair[j].start()
-    t_first = []
-    for j in ORDER:
-        tpair[j].wait_recv()
-        t_sum[j] = (t_rx[j] + work[j, c]).astype(BF16)
-        t_first += first_hop(j, t_sum, t_r1, (t1_send, t1_recv))
+        if n:
+            t_first += teacher_rows(ORDER[n - 1])
+    t_first += teacher_rows(ORDER[-1])
     t_second = [second_hop(h, t_first, t_sum, t_r1, t_r2, (t2_send, t2_recv)) for h in (0, 1)]
 
     s_first[2].wait_recv()
@@ -205,9 +218,9 @@
     s_lse = s_top + jnp.log(s_total)
     cross = sum(e[4:5] * jnp.exp(e[0:1] - t_lse) for e in every)
     kl = cross - t_lse + s_lse
-    kl_ref[...] = jnp.broadcast_to(kl, kl_ref.shape)
     line = lax.broadcasted_iota(jnp.int32, tile.shape, 0)
     tile[...] = jnp.where(line == 0, t_lse, jnp.where(line == 1, s_lse, 0.0)).T
+    kl_mine[...] = jnp.broadcast_to(kl, tile.shape).T
     t_lse = tile[:, 0:1]
     s_lse = tile[:, 1:2]
     me = owner(0, c)
@@ -224,6 +237,23 @@
     for copy in sent:
         copy.start()
 
+    def kl_copy(j):
+        return remote(
+            kl_mine.at[at(mates[j], unit), :], kl_all.at[at(mine_at, unit), :],
+            kl_send.at[j], kl_recv.at[mine_at], (mates[j], high, z),
+        )
+
+    @pl.when(high != c)
+    def _():
+        kl_copy(0).start()
+
+    @pl.when(high == c)
+    def _():
+        kl_all[at(mine_at, unit), :] = kl_mine[at(t, unit), :]
+
+    for j in (1, 2, 3):
+        kl_copy(j).start()
+
     def arrived(j, k, columns=pl.ds(0, cols)):
         g_copy(j, c, chips, k, devs[1], columns).wait_recv()
 
@@ -237,19 +267,24 @@
     def hidden_rows(j):
         g_copy(j, other, cores, j, core).wait_recv()
         where = at(mates[j], 2 * rows)
-        ghp[where, :] = lax.dot_general(
+        part = lax.dot_general(
             g_all[where, :], w_ref[...], (((1,), (1,)), ((), ())), preferred_element_type=F32
         ).astype(BF16)
-        for q in range(Z // 4):
-            target = mates[j] * (Z // 4) + q
-            copy = remote(
-                ghp.at[at(target, hrows)], gh_rx.at[z], gh_send.at[j * (Z // 4) + q], gh_recv.at[z], (t, c, target)
-            )
-            gh_out.append((target, copy))
-
-            @pl.when(target != z)
-            def _(copy=copy):
-                copy.start()
+        for q in range(4):
+            for k in (0, 1):
+                ghp[at(q * 8 + 2 * mates[j] + k, unit), :] = part[k * rows + q * unit:k * rows + (q + 1) * unit]
+            for p in range(2 * unit // piece):
+                first = q * 8 * unit + mates[j] * 2 * unit + p * piece
+                target, inside = lax.div(first, hrows), lax.div(lax.rem(first, hrows), piece)
+                copy = remote(
+                    ghp.at[at(lax.div(first, piece), piece)], gh_rx.at[z, at(inside, piece)],
+                    gh_send.at[len(gh_out)], gh_recv.at[z, inside], (t, c, target),
+                )
+                gh_out.append((target, copy))
+
+                @pl.when(target != z)
+                def _(copy=copy):
+                    copy.start()
 
     arrived(1, 0)
     forward(1, chips, 2, devs[2], cut[0])
@@ -274,12 +309,32 @@
     total = ghp[at(z, hrows), :].astype(F32)
     for dz in range(1, Z):
         source = lax.rem(z + dz, Z)
-        remote(
-            ghp.at[at(source, hrows)], gh_rx.at[source], gh_send.at[0], gh_recv.at[source], (t, c, source)
-        ).wait_recv()
+        for p in range(hrows // piece):
+            where = pl.ds(p * piece, piece)
+            remote(
+                ghp.at[where], gh_rx.at[source, where], gh_send.at[0], gh_recv.at[source, p], (t, c, source)
+            ).wait_recv()
         total = total + gh_rx[source].astype(F32)
     gh_ref[...] = total.astype(BF16)
 
+    for k in range(4):
+        here = (2 * c + k // 2 == t) & (c == k % 2)
+
+        @pl.when(jnp.logical_not(here))
+        def _(k=k):
+            where = pl.ds(k * unit, unit)
+            remote(
+                kl_mine.at[where, :], kl_all.at[where, :], kl_send.at[0], kl_recv.at[k], core
+            ).wait_recv()
+
+    kl_ref[...] = kl_all[...].T[:8, :]
+
+    @pl.when(high != c)
+    def _():
+        kl_copy(0).wait_send()
+
+    for j in (1, 2, 3):
+        kl_copy(j).wait_send()
     for target, copy in gh_out:
         @pl.when(target != z)
         def _(copy=copy):
@@ -303,9 +358,15 @@
     ids = jnp.arange(seqs, dtype=jnp.int32)
     same = (teacher_of_seq[None, :] == teacher_of_seq[:, None]) & (ids[None, :] < ids[:, None])
     zrows, width = teacher_hidden.shape[1:]
-    all_rows = jnp.arange(row_count, dtype=jnp.int32)
-    slot = jnp.repeat(jnp.sum(same.astype(jnp.int32), axis=1), positions) * positions + all_rows % positions
-    live = jnp.repeat(teacher_of_seq == lax.axis_index("teacher"), positions)
+    unit = rows // 4
+    piece = min(2 * unit, row_count // Z)
+    all_rows = jnp.arange(row_count, dtype=jnp.int32).reshape(4, owners, unit)
+    all_rows = all_rows.transpose(1, 0, 2).reshape(row_count)
+    sequence = all_rows // positions
+    chosen = sequence[:, None] == ids[None, :]
+    earlier = jnp.sum(same.astype(jnp.int32), axis=1)
+    slot = jnp.sum(jnp.where(chosen, earlier[None, :], 0), axis=1) * positions + all_rows % positions
+    live = jnp.any(chosen & (teacher_of_seq == lax.axis_index("teacher"))[None, :], axis=1)
     slot_ids = jnp.arange(zrows * Z, dtype=jnp.int32)
     pick = ((slot[:, None] == slot_ids[None, :]) & live[:, None]).astype(BF16)
     hrows = row_count // Z
@@ -333,7 +394,10 @@
             pltpu.VMEM((4, rows, cols), BF16),
             pltpu.VMEM((2, rows, cols), BF16),
             pltpu.VMEM((rows, cols), BF16),
+            pltpu.VMEM((row_count, features), BF16),
             pltpu.VMEM((features, row_count), BF16),
+            pltpu.VMEM((rows, rows), F32),
+            pltpu.VMEM((rows, rows), F32),
             pltpu.VMEM((Z, 8, rows), F32),
             pltpu.VMEM((rows, rows), F32),
             pltpu.VMEM((row_count, cols), BF16),
@@ -341,7 +405,8 @@
             pltpu.VMEM((Z, hrows, features), BF16),
             dma(()), dma((2, Z)), dma((Z,)),
             *hop_sems, *hop_sems,
-            dma((Z,)), dma((Z,)), dma((4,)), dma((4,)), dma((4,)), dma((4,)), dma((Z,)), dma((Z,)),
+            dma((Z,)), dma((Z,)), dma((4,)), dma((4,)), dma((4,)), dma((4,)),
+            dma((row_count // piece,)), dma((Z, hrows // piece)), dma((4,)), dma((4,)),
         ],
         compiler_params=pltpu.CompilerParams(
             collective_id=0, has_side_effects=True, vmem_limit_bytes=60 * 1024 * 1024

time: 126 us -> 121 us (0.960); the launches traced: 126 us -> 119 us
  Pallas kernels: 117 us -> 110 us
    pallas_call x1, Pallas kernels: 117 us -> 110 us  [shards(): pl.pallas_call(functools.partial(kernel, Z, float(cols * Z)), out_shape=(...]
where the time goes in v2:
time: 121 us; the launch traced here: 119 us
  Pallas kernels  110 us (91%)
  local copies, waits for them, and re-layouts  4.72 us (4%)
  other arithmetic  3.38 us (3%)
    pallas_call x1, Pallas kernels, shards(): pl.pallas_call(functools.partial(kernel, Z, float(cols * Z)), out_shape=(...  110 us
    unnamed x4, local copies, waits for them, and re-layouts  3.41 us

profile of v2, /device:TPU:7, one launch (start us, length us, event | category | flops | bytes accessed | tf_op | source)
XLA Modules:
  0.0 119.2 jit_solution(18378509979421462686)
XLA Ops:
  0.6 0.7 broadcast_compare_fusion
  1.3 0.9 convert_reduce_fusion
  2.2 0.1 reshape.117
  2.3 0.1 fusion.3
  2.4 0.1 select_reduce_fusion
  2.5 1.6 %fusion.1.pick_ref = bf16[1024,512]{1,0:T(8,128)(2,1)} fusion(s32[1024]{0:T(1024)S(1)} %fusion.5, pred[1024]{0:T(1024)(128)(4,1)S(1)} %fusion.3), kind=kLoop, calls=%fused_computation.2 | loop fusion | flops 1572864 | bytes 1053696 | tf_op jit(solution)/shard_map/convert_element_type | solution.py:371
  4.1 110.5 %shard_map.76 = (f32[8,128]{1,0:T(8,128)}, bf16[384,2048]{1,0:T(8,128)(2,1)}, bf16[256,384]{1,0:T(8,128)(2,1)}) custom-call(bf16[1024,512]{1,0:T(8,128)(2,1)} %fusion.1.pick_ref, bf16[128,2048]{1,0:T(8,128)(2,1)} %bitcast.5, bf16[2048,2048]{1,0:T(8,128)(2,1)} %bitcast.4, bf16[1024,384]{1,0:T(8,128)(2,1)} %x_ref.1, bf16[384,2048]{1,0:T(8,128)(2,1)} %w_ref.1), custom_call_target="tpu_custom_call" | custom-call | tf_op jit(solution)/shard_map/pallas_call | solution.py:376
  114.6 0.0 copy-start
  114.6 1.2 %slice_bitcast_fusion = f32[128]{0:T(128)} fusion(f32[8,128]{1,0:T(8,128)} %get-tuple-element.6), kind=kLoop, calls=%fused_computation.20 | loop fusion | bytes 1024 | tf_op jit(solution)/shard_map/squeeze | solution.py:415
  115.8 2.7 %copy.10 = bf16[384,2048]{1,0:T(8,128)(2,1)} copy(bf16[384,2048]{1,0:T(8,128)(2,1)} %get-tuple-element.13) | data formatting | bytes 3145728
  118.6 0.0 copy-done
  118.6 0.7 copy.11
  (3 shorter events, 0.0 us)
Async XLA Ops:
  114.6 4.0 %copy-start = (bf16[256,384]{1,0:T(8,128)(2,1)S(1)}, bf16[256,384]{1,0:T(8,128)(2,1)}, u32[]{:S(2)}) copy-start(bf16[256,384]{1,0:T(8,128)(2,1)} %get-tuple-element.14) | copy-start | bytes 589828

commit v3 on v2

--- a/solution.py
+++ b/solution.py
@@ -134,18 +134,21 @@
         pair[j] = remote(work.at[j, other], s_rx.at[j], sc_send.at[j], sc_recv.at[j], core)
         pair[j].start()
     s_first = []
-    for j in ORDER:
+    for n, j in enumerate(ORDER):
+        if n == 3:
+            z_wait(0)
+            z_start(1)
         mine = jnp.dot(xp[at(owner(j, c), rows), :], w_ref[...], preferred_element_type=F32)
         pair[j].wait_recv()
         s_rx[j] = s_rx[j] + mine
         s_first += first_hop(j, s_rx, s_r1, (s1_send, s1_recv))
-    xt[...] = xp[...].T
-    for step in range(Z - 1):
+    s_second = [second_hop(h, s_first, s_rx, s_r1, s_r2, (s2_send, s2_recv)) for h in (0, 1)]
+    for step in range(1, Z - 1):
         z_wait(step)
         if step + 1 < Z - 1:
             z_start(step + 1)
-        if step == 0:
-            s_second = [second_hop(h, s_first, s_rx, s_r1, s_r2, (s2_send, s2_recv)) for h in (0, 1)]
+        if step == 1:
+            xt[...] = xp[...].T
     head_copy.wait()
 
     for j in ORDER:

time: 121 us -> 121 us (level)
  no operation moved by 1% of the time
where the time goes in v3:
time: 121 us; the launch traced here: 119 us
  Pallas kernels  110 us (91%)
  local copies, waits for them, and re-layouts  4.72 us (4%)
  other arithmetic  3.38 us (3%)
    pallas_call x1, Pallas kernels, shards(): pl.pallas_call(functools.partial(kernel, Z, float(cols * Z)), out_shape=(...  110 us
    unnamed x4, local copies, waits for them, and re-layouts  3.41 us

profile of v3, /device:TPU:7, one launch (start us, length us, event | category | flops | bytes accessed | tf_op | source)
XLA Modules:
  0.0 119.2 jit_solution(17542655171699527164)
XLA Ops:
  0.6 0.7 broadcast_compare_fusion
  1.3 0.9 convert_reduce_fusion
  2.2 0.1 reshape.117
  2.3 0.1 fusion.3
  2.4 0.1 select_reduce_fusion
  2.5 1.6 %fusion.1.pick_ref = bf16[1024,512]{1,0:T(8,128)(2,1)} fusion(s32[1024]{0:T(1024)S(1)} %fusion.5, pred[1024]{0:T(1024)(128)(4,1)S(1)} %fusion.3), kind=kLoop, calls=%fused_computation.2 | loop fusion | flops 1572864 | bytes 1053696 | tf_op jit(solution)/shard_map/convert_element_type | solution.py:374
  4.1 110.5 %shard_map.76 = (f32[8,128]{1,0:T(8,128)}, bf16[384,2048]{1,0:T(8,128)(2,1)}, bf16[256,384]{1,0:T(8,128)(2,1)}) custom-call(bf16[1024,512]{1,0:T(8,128)(2,1)} %fusion.1.pick_ref, bf16[128,2048]{1,0:T(8,128)(2,1)} %bitcast.5, bf16[2048,2048]{1,0:T(8,128)(2,1)} %bitcast.4, bf16[1024,384]{1,0:T(8,128)(2,1)} %x_ref.1, bf16[384,2048]{1,0:T(8,128)(2,1)} %w_ref.1), custom_call_target="tpu_custom_call" | custom-call | tf_op jit(solution)/shard_map/pallas_call | solution.py:379
  114.6 0.0 copy-start
  114.6 1.2 %slice_bitcast_fusion = f32[128]{0:T(128)} fusion(f32[8,128]{1,0:T(8,128)} %get-tuple-element.6), kind=kLoop, calls=%fused_computation.20 | loop fusion | bytes 1024 | tf_op jit(solution)/shard_map/squeeze | solution.py:418
  115.8 2.7 %copy.10 = bf16[384,2048]{1,0:T(8,128)(2,1)} copy(bf16[384,2048]{1,0:T(8,128)(2,1)} %get-tuple-element.13) | data formatting | bytes 3145728
  118.5 0.0 copy-done
  118.5 0.7 copy.11
  (3 shorter events, 0.0 us)
Async XLA Ops:
  114.6 4.0 %copy-start = (bf16[256,384]{1,0:T(8,128)(2,1)S(1)}, bf16[256,384]{1,0:T(8,128)(2,1)}, u32[]{:S(2)}) copy-start(bf16[256,384]{1,0:T(8,128)(2,1)} %get-tuple-element.14) | copy-start | bytes 589828
